TPU v7x, 32 devices: a whole 2x2x4 slice. The times are simulated.
32 devices in a mesh: member: 2 (over x), lat: 16 (over z, y, core).
Axes of the slice: x: 2, y: 2, z: 4, core: 2. Of those that a mesh axis runs over, the one named last changes fastest.
Arguments:
- state: float32 [10, 128, 128, 256], P('member', None, 'lat'), parts along dimension 0, may hold values from -6 to 6
- wind: float32 [256, 128, 256], P('member', 'lat'), parts along dimension 0, may hold values from -0.9 to 0.9
- sunlight: float32 [256, 256], P(('member', 'lat')), parts along dimension 0, may hold values from 0.1 to 1
- day_list: int32 [32, 16], P(('member', 'lat')), parts along dimension 0, may hold values from -1 to 15, as said below
- w_first: bfloat16 [640, 2048], replicated, may hold values from -0.25 to 0.25
- bias: float32 [2048], replicated, may hold values from -3 to 3
- w_second: bfloat16 [2048, 128], replicated, may hold values from -0.125 to 0.125
- remap: float32 [128, 128], replicated, may hold values from -1.5 to 2
Outputs:
- new_state: float32 [10, 128, 128, 256], P('member', None, 'lat'), parts along dimension 0
There are 2 independent parts, one for each index of `member`. A program takes and returns all parts, laid end to end along the dimension named above; an argument that names none is the same for every part. Nothing has to cross between parts.
Inputs may be any that keep to these rules, and one draw needn't show every extreme that they name: `day_list`: row d names the daylit blocks of band d, each once, as a cyclic run of consecutive numbers placed first, then -1; every row names at least one block. Rows d and d + 8 together name at most 20 blocks; row 0 names all 16 and row 8 exactly 4.
All inputs are finite; a program needn't handle non-finite values.
Results may differ from a plain program's by a relative error of at most 0.00062.
Values may be sent and summed in bfloat16 or wider, within the bound.
A program may use at most 128 MiB of HBM per device.

v0:
```python
import functools

import jax
import jax.numpy as jnp
from jax import lax
from jax.experimental import pallas as pl
from jax.experimental.pallas import tpu as pltpu
from jax.sharding import PartitionSpec as P

STEPS = 2
REACH = 2 * STEPS
SCALE = 4096.0
FACES = 3
PARTS = 2
CHUNKS = 4
TILES = 4
MIB = 1 << 20


def pack_kernel(flags, state_ref, wind_ref, own_ref, near_ref, *far_refs):
    fields, levels, parts, rows, width = state_ref.shape
    flat = state_ref.reshape(fields * levels * parts * rows, width)
    winds = wind_ref.reshape(levels * parts * rows, width)
    odd = flags[0]
    for part in range(parts):
        for j in range(rows):
            for f in range(fields):
                start = (f * levels * parts + part) * rows + j
                own_ref[part, j * fields + f] = flat[pl.ds(start, levels, stride=parts * rows), :]
            start = part * rows + j
            own_ref[part, rows * fields + j] = winds[pl.ds(start, levels, stride=parts * rows), :]

    def send(upward):
        state_row = rows - REACH if upward else 0
        wind_row = rows - FACES if upward else 0

        def slab(part, n):
            if n < REACH * fields:
                return own_ref[part, state_row * fields + n]
            return own_ref[part, rows * fields + wind_row + n - REACH * fields]

        return slab

    down, up = send(False), send(True)
    for far_slab, near_slab, chosen in ((up, down, odd == 1), (down, up, odd == 0)):

        @pl.when(chosen)
        def _():
            for part in range(PARTS):
                for n in range(REACH * fields + FACES):
                    far_refs[part][n] = far_slab(part, n) * SCALE
                    near_ref[part, n] = near_slab(part, n)


def parted(x):
    *outer, rows, lons = x.shape
    return jnp.swapaxes(x.reshape(*outer, rows, PARTS, lons // PARTS), -3, -2)


def pack(flags, state, wind):
    fields, levels, rows, lons = state.shape
    width = lons // PARTS
    step = levels // CHUNKS
    sent = REACH * fields + FACES
    own = rows * (fields + 1)
    whole = lambda i, s: (0, 0, i, 0)
    return pl.pallas_call(
        pack_kernel,
        grid_spec=pltpu.PrefetchScalarGridSpec(
            num_scalar_prefetch=1,
            grid=(CHUNKS,),
            in_specs=[
                pl.BlockSpec((fields, step, PARTS, rows, width), lambda i, s: (0, i, 0, 0, 0)),
                pl.BlockSpec((step, PARTS, rows, width), lambda i, s: (i, 0, 0, 0)),
            ],
            out_specs=[
                pl.BlockSpec((PARTS, own, step, width), whole),
                pl.BlockSpec((PARTS, sent, step, width), whole),
            ]
            + [pl.BlockSpec((sent, step, width), lambda i, s: (0, i, 0))] * PARTS,
        ),
        out_shape=[
            jax.ShapeDtypeStruct((PARTS, own, levels, width), jnp.float32),
            jax.ShapeDtypeStruct((PARTS, sent, levels, width), jnp.float32),
        ]
        + [jax.ShapeDtypeStruct((sent, levels, width), jnp.float32)] * PARTS,
        name="pack",
        compiler_params=pltpu.CompilerParams(vmem_limit_bytes=24 * MIB),
        cost_estimate=pl.CostEstimate(flops=10**6, bytes_accessed=18 * 10**6, transcendentals=0),
    )(flags, parted(state), parted(wind))


def limited(left, right):
    return jnp.maximum(jnp.minimum(left, right), 0.0) + jnp.minimum(jnp.maximum(left, right), 0.0)


def advance(q, c, ck, positive, first, last):
    diff = {j: q[j + 1] - q[j] for j in range(first - 2, last + 2)}
    slope = {j: limited(diff[j], diff[j - 1]) for j in range(first - 1, last + 2)}
    flux = {}
    for j in range(first, last + 2):
        flux[j] = c[j] * jnp.where(positive[j], q[j - 1], q[j]) + ck[j] * jnp.where(
            positive[j], slope[j - 1], slope[j]
        )
    return {j: q[j] - (flux[j + 1] - flux[j]) for j in range(first, last + 1)}


def gelu(v):
    inner = v * (0.7978845608028654 + (0.7978845608028654 * 0.044715) * (v * v))
    half = 0.5 * v
    return (half + half * jnp.tanh(inner)).astype(jnp.bfloat16)


def advect_rows(north, inner, rows, fields, own_ref, halo, adv, offset):
    chunk = own_ref.shape[2]
    slabs = REACH * fields
    first = 0 if north else rows - REACH
    last = first + REACH - 1

    @pl.loop(0, chunk // 8)
    def _(t):
        here = pl.ds(pl.multiple_of(t * 8, 8), 8)
        there = pl.ds(pl.multiple_of(offset + t * 8, 8), 8)
        c = {}
        for j in range(first - 2, last + 4):
            if j < 0:
                c[j] = halo(slabs + FACES + j, here)
            elif j < rows:
                c[j] = own_ref[0, rows * fields + j, here, :]
            else:
                c[j] = halo(slabs + j - rows, here)
        positive = {j: v > 0.0 for j, v in c.items()}
        ck = {j: 0.5 * (jnp.abs(v) - v * v) for j, v in c.items()}
        for f in range(fields):
            q = {}
            for j in range(first - REACH, last + REACH + 1):
                if j < 0:
                    q[j] = halo((j + REACH) * fields + f, here)
                elif j < rows:
                    q[j] = own_ref[0, j * fields + f, here, :]
                else:
                    q[j] = halo((j - rows) * fields + f, here)
            q = advance(q, c, ck, positive, first - 2, last + 2)
            if north:
                q[-1] = q[-1] * inner
                q[-2] = q[-2] * inner
            q = advance(q, c, ck, positive, first, last)
            for j in range(REACH):
                adv[j, f, there, :] = q[first + j]


def main_kernel(slow, part, rows, flags, own_ref, halo_ref, sun_ref, bias_ref, remap_ref, w1_hbm, w2_hbm, *rest):
    if slow:
        out_hbm, adv, x16, w1, w2, sems, result = rest[-7:]
        fast_ref = rest[0]
    else:
        out_ref, unscale_ref, adv, x16, w1, w2, sems = rest[-7:]
        unscale_ref[0] = 1.0 / SCALE
    half = pl.program_id(0)
    step_id = pl.program_id(1)
    chunk = own_ref.shape[2]
    reach, fields, levels, lons = adv.shape
    load_1 = pltpu.make_async_copy(w1_hbm, w1, sems.at[0])
    load_2 = pltpu.make_async_copy(w2_hbm, w2, sems.at[1])
    odd = flags[flags.shape[0] - 2]
    north = 1 - odd if slow else odd
    inner = jnp.where(flags[flags.shape[0] - 1] > 0, 1.0, 0.0)
    offset = step_id * chunk

    def halo(n, here):
        return halo_ref[n, here, :] if slow else halo_ref[0, n, here, :]

    @pl.when((step_id == 0) & (half == 0))
    def _():
        load_1.start()
        load_2.start()

    @pl.when((step_id < CHUNKS) & (north == 1))
    def _():
        advect_rows(True, inner, rows, fields, own_ref, halo, adv, offset)

    @pl.when((step_id < CHUNKS) & (north == 0))
    def _():
        advect_rows(False, inner, rows, fields, own_ref, halo, adv, offset)

    @pl.when((step_id == CHUNKS) & (half == 0))
    def _():
        load_1.wait()
        load_2.wait()

    @pl.when(step_id == CHUNKS)
    def _():
        base = (1 - north) * (rows - REACH)
        if slow:
            flat_out = result.reshape(fields * levels * rows, lons)
            fast_base = north * (rows - REACH)
            columns = pl.ds(part * lons, lons)
            heated = pl.ds(0, 1)
            others = pl.ds(1, fields - 1)
            store_others = pltpu.make_async_copy(
                result.at[others], out_hbm.at[others, :, :, columns], sems.at[2])
            store_heated = pltpu.make_async_copy(
                result.at[heated], out_hbm.at[heated, :, :, columns], sems.at[3])

        def put(k, f, values):
            if slow:
                flat_out[pl.ds(f * levels * rows + base + k, levels, stride=rows), :] = values
            else:
                out_ref[0, k, f] = values

        remap = remap_ref[...]
        r_high = remap.astype(jnp.bfloat16)
        r_low = (remap - r_high.astype(jnp.float32)).astype(jnp.bfloat16)
        r_all = jnp.concatenate([r_high, r_low, r_high], axis=1)
        hidden_size = w1.shape[0]
        tile = hidden_size // TILES

        for f in range(fields):
            for pair in range(REACH // 2):
                a, b = 2 * pair, 2 * pair + 1
                x = jnp.concatenate([adv[a, f], adv[b, f]], axis=1)
                high = x.astype(jnp.bfloat16)
                low = (x - high.astype(jnp.float32)).astype(jnp.bfloat16)
                stacked = jnp.concatenate([high, high, low], axis=0)
                y = jnp.dot(r_all, stacked, preferred_element_type=jnp.float32)
                x16[pair, pl.ds(f * levels, levels), :] = y.astype(jnp.bfloat16)
                if f == 0:
                    adv[a, 0] = y[:, :lons]
                    adv[b, 0] = y[:, lons:]
                else:
                    put(a, f, y[:, :lons])
                    put(b, f, y[:, lons:])
        if slow:
            for k in range(REACH):
                for f in range(fields):
                    place = pl.ds(f * levels * rows + fast_base + k, levels, stride=rows)
                    flat_out[place, :] = fast_ref[0, k, f]
            store_others.start()

        for pair in range(REACH // 2):
            a, b = 2 * pair, 2 * pair + 1
            lit_a = flags[PARTS * (base + a) + part + half]
            lit_b = flags[PARTS * (base + b) + part + half]

            @pl.when(lit_a + lit_b > 0)
            def _():
                inputs = x16[pair]

                def layer(t):
                    z = jnp.dot(w1[pl.ds(t * tile, tile), :], inputs,
                                preferred_element_type=jnp.float32)
                    wide = bias_ref[pl.ds(t * tile, tile), :]
                    return z + jnp.concatenate([wide, wide], axis=1)

                net = jnp.zeros((levels, 2 * lons), jnp.float32)
                z = layer(0)
                for t in range(TILES):
                    later = layer(t + 1) if t < TILES - 1 else None
                    net = net + jnp.dot(w2[:, pl.ds(t * tile, tile)], gelu(z),
                                        preferred_element_type=jnp.float32)
                    z = later
                for k, lit, values in ((a, lit_a, net[:, :lons]), (b, lit_b, net[:, lons:])):
                    weight = sun_ref[pl.ds(base + k, 1), :] * jnp.where(lit > 0, 1.0, 0.0)
                    adv[k, 0] = adv[k, 0] + weight * values

        for k in range(REACH):
            put(k, 0, adv[k, 0])
        if slow:
            store_heated.start()
            store_others.wait()
            store_heated.wait()


def compute(slow, part, flags, own, halo, sunlight, bias, remap, w1, w2, fast=None, before=None):
    rows, lons = sunlight.shape
    levels, width = own.shape[2:]
    fields = own.shape[1] // rows - 1
    step = levels // CHUNKS
    last = CHUNKS - 1
    hidden_size = w1.shape[0]
    any_spec = pl.BlockSpec(memory_space=pl.ANY)
    halves = 1 if slow else PARTS
    if slow:
        halo_spec = pl.BlockSpec((halo.shape[0], step, width), lambda h, i, s: (0, jnp.minimum(i, last), 0))
    else:
        halo_spec = pl.BlockSpec((1, halo.shape[1], step, width), lambda h, i, s: (h, 0, jnp.minimum(i, last), 0))
    in_specs = [
        pl.BlockSpec((1, own.shape[1], step, width), lambda h, i, s: (part + h, 0, jnp.minimum(i, last), 0)),
        halo_spec,
        pl.BlockSpec((rows, width), lambda h, i, s: (0, part + h)),
        pl.BlockSpec((hidden_size, width), lambda h, i, s: (0, 0)),
        pl.BlockSpec((levels, levels), lambda h, i, s: (0, 0)),
        any_spec,
        any_spec,
    ]
    operands = [flags, own, halo, sunlight, bias, remap, w1, w2]
    scratch = [
        pltpu.VMEM((REACH, fields, levels, width), jnp.float32),
        pltpu.VMEM((REACH // 2, fields * levels, 2 * width), jnp.bfloat16),
        pltpu.VMEM(w1.shape, jnp.bfloat16),
        pltpu.VMEM(w2.shape, jnp.bfloat16),
        pltpu.SemaphoreType.DMA((4,)),
    ]
    aliases = {}
    if slow:
        in_specs.append(pl.BlockSpec((1, REACH, fields, levels, width), lambda h, i, s: (part, 0, 0, 0, 0)))
        operands.append(fast)
        out_spec = any_spec
        out_shape = jax.ShapeDtypeStruct((fields, levels, rows, lons), jnp.float32)
        scratch.append(pltpu.VMEM((fields, levels, rows, width), jnp.float32))
        if before is not None:
            in_specs.append(any_spec)
            operands.append(before)
            aliases = {len(operands) - 1: 0}
    else:
        out_spec = [
            pl.BlockSpec((1, REACH, fields, levels, width), lambda h, i, s: (h, 0, 0, 0, 0)),
            pl.BlockSpec(memory_space=pltpu.SMEM),
        ]
        out_shape = [
            jax.ShapeDtypeStruct((PARTS, REACH, fields, levels, width), jnp.float32),
            jax.ShapeDtypeStruct((1,), jnp.float32),
        ]
    return pl.pallas_call(
        functools.partial(main_kernel, slow, part, rows),
        grid_spec=pltpu.PrefetchScalarGridSpec(
            num_scalar_prefetch=1,
            grid=(halves, CHUNKS + 1),
            in_specs=in_specs,
            out_specs=out_spec,
            scratch_shapes=scratch,
        ),
        out_shape=out_shape,
        input_output_aliases=aliases,
        name="slow_rows" if slow else "fast_rows",
        compiler_params=pltpu.CompilerParams(vmem_limit_bytes=36 * MIB),
        cost_estimate=pl.CostEstimate(
            flops=2 * 10**9 * halves, bytes_accessed=6 * 10**6 * halves, transcendentals=10**6 * halves
        ),
    )(*operands)


def shards(state, wind, sunlight, day_list, w_first, bias, w_second, remap):
    count = lax.axis_size("lat")
    near = [(i, i ^ 1) for i in range(count) if i ^ 1 < count]
    far = [(i, i + 1) for i in range(1, count - 1, 2)]
    far = far + [(j, i) for i, j in far]
    index = lax.axis_index("lat")
    blocks = day_list.shape[1]
    block_ids = jnp.arange(blocks, dtype=jnp.int32)
    lit = jnp.any(day_list[0][None, :] == block_ids[:, None], axis=1).astype(jnp.int32)
    odd = (index % 2).astype(jnp.int32)
    inner = (index > 0).astype(jnp.int32)
    flags = jnp.concatenate([lit, odd[None], inner[None]])
    side = jnp.stack([odd, inner])
    own, near_sent, *far_sent = pack(side, state, wind)
    far_halos = [lax.ppermute(sent.astype(jnp.float16), "lat", far) for sent in far_sent]
    near_halo = lax.ppermute(near_sent, "lat", near)
    w1, w2 = w_first.T, w_second.T
    wide_bias = jnp.broadcast_to(bias[:, None], (bias.shape[0], state.shape[3] // PARTS))
    shared = (sunlight, wide_bias, remap, w1, w2)
    fast, unscale = compute(False, 0, flags, own, near_halo, *shared)
    out = None
    for part in range(PARTS):
        halo = far_halos[part].astype(jnp.float32) * unscale[0]
        out = compute(True, part, flags, own, halo, *shared, fast=fast, before=out)
    return out


def solution(mesh):
    placed = (
        P("member", None, "lat", None),
        P("member", "lat", None),
        P(("member", "lat"), None),
        P(("member", "lat"), None),
        P(),
        P(),
        P(),
        P(),
    )
    return jax.shard_map(
        shards,
        mesh=mesh,
        in_specs=placed,
        out_specs=P("member", None, "lat", None),
        check_vma=False,
    )
```

profile of v0, /device:TPU:1, one launch (start us, length us, event | category | flops | bytes accessed | tf_op | source)
XLA Modules:
  0.0 65.2 jit_solution(319420677537888411)
XLA Ops:
  0.0 0.1 pad_add_fusion.1.flags
  0.1 0.0 copy-start.2
  0.1 2.5 %copy-done.2 = f32[5,128,8,256]{3,2,1,0:T(8,128)S(1)} copy-done((f32[5,128,8,256]{3,2,1,0:T(8,128)S(1)}, f32[5,128,8,256]{3,2,1,0:T(8,128)}, u32[]{:S(2)}) %copy-start.2) | copy-done | bytes 5242904
  2.6 0.0 copy-start.3
  2.6 1.2 %copy-done.3 = f32[128,8,256]{2,1,0:T(8,128)S(1)} copy-done((f32[128,8,256]{2,1,0:T(8,128)S(1)}, f32[128,8,256]{2,1,0:T(8,128)}, u32[]{:S(2)}) %copy-start.3) | copy-done | bytes 1048600
  3.8 5.2 %pack.1 = (f32[2,48,128,128]{3,2,1,0:T(8,128)S(1)}, f32[2,23,128,128]{3,2,1,0:T(8,128)}, f32[23,128,128]{2,1,0:T(8,128)S(1)}, f32[23,128,128]{2,1,0:T(8,128)S(1)}) custom-call(s32[2]{0:T(128)S(1)} %pad_add_fusion.1.flags, f32[5,128,2,8,128]{4,3,2,1,0:T(8,128)S(1)} %bitcast.15, f32[128,2,8,128]{3,2,1,0:T(8,128)S(1)} %bitcast.19), custom_call_target="tpu_custom_call" | custom-call | flops 1000000 | bytes 18000000 | tf_op jit(solution)/shard_map/pack/pallas_call | solution.py:67
  9.0 0.0 copy-start
  9.0 2.7 %copy-done = f32[2,48,128,128]{3,2,1,0:T(8,128)} copy-done((f32[2,48,128,128]{3,2,1,0:T(8,128)}, f32[2,48,128,128]{3,2,1,0:T(8,128)S(1)}, u32[]{:S(2)}) %copy-start) | copy-done | bytes 6291480
  11.6 0.1 collective-permute-start.1
  11.7 1.0 %convert_element_type.19 = f16[23,128,128]{2,1,0:T(8,128)(2,1)} convert(f32[23,128,128]{2,1,0:T(8,128)S(1)} %get-tuple-element.16) | non-fusion elementwise | flops 376832 | bytes 2260992 | tf_op jit(solution)/shard_map/convert_element_type | solution.py:357
  12.8 0.0 copy-start.8
  12.8 0.0 copy-start.6
  12.8 4.6 %collective-permute-start.2 = (f16[23,128,128]{2,1,0:T(8,128)(2,1)}, f16[23,128,128]{2,1,0:T(8,128)(2,1)}, u32[]{:S(2)}, u32[]{:S(2)}) collective-permute-start(f16[23,128,128]{2,1,0:T(8,128)(2,1)} %convert_element_type.19), channel_id=1, source_target_pairs={{1,2},{3,4},{5,6},{7,8},{9,10},{11,12},{13,14},{2,1},{4,3},{6,5},{... | collective-permute-start | bytes 2261000 | tf_op jit(solution)/shard_map/ppermute | solution.py:357
  17.4 1.0 %convert_element_type.17 = f16[23,128,128]{2,1,0:T(8,128)(2,1)} convert(f32[23,128,128]{2,1,0:T(8,128)S(1)} %get-tuple-element.12) | non-fusion elementwise | flops 376832 | bytes 2260992 | tf_op jit(solution)/shard_map/convert_element_type | solution.py:357
  18.4 1.9 %collective-permute-start = (f16[23,128,128]{2,1,0:T(8,128)(2,1)}, f16[23,128,128]{2,1,0:T(8,128)(2,1)}, u32[]{:S(2)}, u32[]{:S(2)}) collective-permute-start(f16[23,128,128]{2,1,0:T(8,128)(2,1)} %convert_element_type.17), channel_id=1, source_target_pairs={{1,2},{3,4},{5,6},{7,8},{9,10},{11,12},{13,14},{2,1},{4,3},{6,5},{... | collective-permute-start | bytes 2261000 | tf_op jit(solution)/shard_map/ppermute | solution.py:357
  20.3 0.0 copy-done.8
  20.3 0.1 fusion
  20.4 0.0 copy-done.6
  20.4 0.2 copy.13
  20.7 0.0 copy-start.7
  20.7 0.0 copy-start.4
  20.7 0.0 copy-start.5
  20.7 3.2 %copy.12 = bf16[640,2048]{0,1:T(8,128)(2,1)S(1)} copy(bf16[640,2048]{1,0:T(8,128)(2,1)} %param.12) | data formatting | bytes 5242880 | tf_op args[4]
  23.9 0.1 pad_add_fusion.flags
  24.0 0.0 collective-permute-done.1.halo_ref
  24.0 0.0 copy-done.7
  24.0 0.3 broadcast_in_dim.19.bias_ref
  24.3 0.0 copy-done.4
  24.3 0.0 copy-done.5
  24.3 0.0 copy-start.1
  24.3 2.8 %copy-done.1 = f32[2,48,128,128]{3,2,1,0:T(8,128)S(1)} copy-done((f32[2,48,128,128]{3,2,1,0:T(8,128)S(1)}, f32[2,48,128,128]{3,2,1,0:T(8,128)}, u32[]{:S(2)}) %copy-start.1) | copy-done | bytes 6291480
  27.1 16.6 %fast_rows.1 = (f32[2,4,5,128,128]{4,3,2,1,0:T(8,128)S(1)}, f32[1]{0:T(128)}) custom-call(s32[18]{0:T(128)S(1)} %pad_add_fusion.flags, f32[2,48,128,128]{3,2,1,0:T(8,128)S(1)} %copy-done.1, f32[2,23,128,128]{3,2,1,0:T(8,128)} %collective-permute-done.1.halo_ref, f32[8,256]{1,0:T(8,128)S(1)} %copy-done.5, f32[2048,128]{1,0:T(8,128)S(1)} %broadcast_in_dim.19.bias_ref, ...), custom_call_target="tpu_custom_call" | custom-call | flops 4000000000 | bytes 12000000 | tf_op jit(solution)/shard_map/fast_rows/pallas_call | solution.py:324
  43.8 0.0 collective-permute-done.2
  43.8 1.9 %convert_multiply_fusion.halo_ref = f32[23,128,128]{2,1,0:T(8,128)S(1)} fusion(f16[23,128,128]{2,1,0:T(8,128)(2,1)} %collective-permute-done.2, f32[]{:T(128)} %bitcast.9), kind=kLoop, calls=%fused_computation | loop fusion | flops 753664 | bytes 2260996 | tf_op jit(solution)/shard_map/mul | solution.py:365
  45.6 8.8 %slow_rows.2.rest_1_ = f32[5,128,8,256]{3,2,1,0:T(8,128)} custom-call(s32[18]{0:T(128)S(1)} %pad_add_fusion.flags, f32[2,48,128,128]{3,2,1,0:T(8,128)S(1)} %copy-done.1, f32[23,128,128]{2,1,0:T(8,128)S(1)} %convert_multiply_fusion.halo_ref, f32[8,256]{1,0:T(8,128)S(1)} %copy-done.5, f32[2048,128]{1,0:T(8,128)S(1)} %broadcast_in_dim.19.bias_ref, ...), custom_call_target="tpu_custom_call" | custom-call | flops 2000000000 | bytes 6000000 | tf_op jit(solution)/shard_map/slow_rows/pallas_call | solution.py:324
  54.5 0.0 collective-permute-done
  54.5 1.9 %convert_multiply_fusion.1.halo_ref = f32[23,128,128]{2,1,0:T(8,128)S(1)} fusion(f16[23,128,128]{2,1,0:T(8,128)(2,1)} %collective-permute-done, f32[]{:T(128)} %bitcast.9), kind=kLoop, calls=%fused_computation.1 | loop fusion | flops 753664 | bytes 2260996 | tf_op jit(solution)/shard_map/mul | solution.py:365
  56.4 8.8 %slow_rows.3 = f32[5,128,8,256]{3,2,1,0:T(8,128)} custom-call(s32[18]{0:T(128)S(1)} %pad_add_fusion.flags, f32[2,48,128,128]{3,2,1,0:T(8,128)S(1)} %copy-done.1, f32[23,128,128]{2,1,0:T(8,128)S(1)} %convert_multiply_fusion.1.halo_ref, f32[8,256]{1,0:T(8,128)S(1)} %copy-done.5, ...), custom_call_target="tpu_custom_call", output_to_operand_aliasing={{}: (9, {})} | custom-call | flops 2000000000 | bytes 6000000 | tf_op jit(solution)/shard_map/slow_rows/pallas_call | solution.py:324
  (1 shorter events, 0.0 us)
Async XLA Ops:
  0.1 2.5 %copy-start.2 = (f32[5,128,8,256]{3,2,1,0:T(8,128)S(1)}, f32[5,128,8,256]{3,2,1,0:T(8,128)}, u32[]{:S(2)}) copy-start(f32[5,128,8,256]{3,2,1,0:T(8,128)} %param.8) | copy-start | bytes 15728644
  2.6 1.2 %copy-start.3 = (f32[128,8,256]{2,1,0:T(8,128)S(1)}, f32[128,8,256]{2,1,0:T(8,128)}, u32[]{:S(2)}) copy-start(f32[128,8,256]{2,1,0:T(8,128)} %param.9) | copy-start | bytes 3145732
  9.0 2.7 %copy-start = (f32[2,48,128,128]{3,2,1,0:T(8,128)}, f32[2,48,128,128]{3,2,1,0:T(8,128)S(1)}, u32[]{:S(2)}) copy-start(f32[2,48,128,128]{3,2,1,0:T(8,128)S(1)} %get-tuple-element.11.own_ref) | copy-start | bytes 18874372
  11.6 12.3 %collective-permute-start.1 = (f32[2,23,128,128]{3,2,1,0:T(8,128)}, f32[2,23,128,128]{3,2,1,0:T(8,128)}, u32[]{:S(2)}, u32[]{:S(2)}) collective-permute-start(f32[2,23,128,128]{3,2,1,0:T(8,128)} %get-tuple-element.13), channel_id=1, source_target_pairs={{0,1},{1,0},{2,3},{3,2},{4,5},{5,4},{6,7},{7,6},{8,9},{9,8},{10,11... | collective-permute-start | bytes 9043976 | tf_op jit(solution)/shard_map/ppermute | solution.py:358
  12.8 7.6 %copy-start.8 = (s32[1,16]{1,0:T(1,128)S(1)}, s32[1,16]{1,0:T(1,128)}, u32[]{:S(2)}) copy-start(s32[1,16]{1,0:T(1,128)} %param.11) | copy-start | bytes 196
  12.8 7.7 %copy-start.6 = (bf16[2048,128]{1,0:T(8,128)(2,1)S(1)}, bf16[2048,128]{1,0:T(8,128)(2,1)}, u32[]{:S(2)}) copy-start(bf16[2048,128]{1,0:T(8,128)(2,1)} %param.14) | copy-start | bytes 1572868
  12.8 31.0 %collective-permute-start.2 = (f16[23,128,128]{2,1,0:T(8,128)(2,1)}, f16[23,128,128]{2,1,0:T(8,128)(2,1)}, u32[]{:S(2)}, u32[]{:S(2)}) collective-permute-start(f16[23,128,128]{2,1,0:T(8,128)(2,1)} %convert_element_type.19), channel_id=1, source_target_pairs={{1,2},{3,4},{5,6},{7,8},{9,10},{11,12},{13,14},{2,1},{4,3},{6,5},{... | collective-permute-start | bytes 2261000 | tf_op jit(solution)/shard_map/ppermute | solution.py:357
  18.4 36.1 %collective-permute-start = (f16[23,128,128]{2,1,0:T(8,128)(2,1)}, f16[23,128,128]{2,1,0:T(8,128)(2,1)}, u32[]{:S(2)}, u32[]{:S(2)}) collective-permute-start(f16[23,128,128]{2,1,0:T(8,128)(2,1)} %convert_element_type.17), channel_id=1, source_target_pairs={{1,2},{3,4},{5,6},{7,8},{9,10},{11,12},{13,14},{2,1},{4,3},{6,5},{... | collective-permute-start | bytes 2261000 | tf_op jit(solution)/shard_map/ppermute | solution.py:357
  20.7 3.3 %copy-start.7 = (f32[2048]{0:T(1024)S(1)}, f32[2048]{0:T(1024)}, u32[]{:S(2)}) copy-start(f32[2048]{0:T(1024)} %param.13) | copy-start | bytes 24580
  20.7 3.6 %copy-start.4 = (f32[128,128]{1,0:T(8,128)S(1)}, f32[128,128]{1,0:T(8,128)}, u32[]{:S(2)}) copy-start(f32[128,128]{1,0:T(8,128)} %remap_ref.5) | copy-start | bytes 196612
  20.7 3.6 %copy-start.5 = (f32[8,256]{1,0:T(8,128)S(1)}, f32[8,256]{1,0:T(8,128)}, u32[]{:S(2)}) copy-start(f32[8,256]{1,0:T(8,128)} %sun_ref.5) | copy-start | bytes 24580
  24.3 2.8 %copy-start.1 = (f32[2,48,128,128]{3,2,1,0:T(8,128)S(1)}, f32[2,48,128,128]{3,2,1,0:T(8,128)}, u32[]{:S(2)}) copy-start(f32[2,48,128,128]{3,2,1,0:T(8,128)} %copy-done) | copy-start | bytes 18874372
where the time goes:
time: 66 us; the launch traced here: 65.2 us
  Pallas kernels  39.5 us (60%)
  local copies, waits for them, and re-layouts  12.9 us (20%)
  starting transfers between devices  6.59 us (10%)
  other arithmetic  6.07 us (9%)
    pallas_call x3, Pallas kernels, compute(): pl.pallas_call(functools.partial(main_kernel, slow, part, rows), grid_spe...  34.3 us
    unnamed x20, local copies, waits for them, and re-layouts  12.5 us
    ppermute x2, starting transfers between devices, shards(): lax.ppermute(sent.astype(jnp.float16), 'lat', far)  6.51 us
    pallas_call x1, Pallas kernels, pack(): pl.pallas_call(pack_kernel, grid_spec=pltpu.PrefetchScalarGridSpec(num_sc...  5.2 us
    mul x2, other arithmetic, shards(): halo = far_halos[part].astype(jnp.float32) * unscale[0]  3.74 us
    convert_element_type x2, other arithmetic, shards(): sent.astype(jnp.float16)  2.05 us
  transfers between devices with their start and end apart: 3, of which 0 were waited for; matrix products, arithmetic and copies ran while one was open for 12% of the time, Pallas kernels for 39%

commit v1 on v0

v1 whole, which is shorter than its diff:
```python
import functools

import jax
import jax.numpy as jnp
from jax import lax
from jax.experimental import pallas as pl
from jax.experimental.pallas import tpu as pltpu
from jax.sharding import PartitionSpec as P

STEPS = 2
REACH = 2 * STEPS
SCALE = 4096.0
FACES = 3
PARTS = 2
CHUNKS = 4
TILES = 4
MIB = 1 << 20


def pack_kernel(flags, state_ref, wind_ref, near_ref, far_ref):
    fields, levels, parts, rows, width = state_ref.shape
    flat = state_ref.reshape(fields * levels * parts * rows, width)
    winds = wind_ref.reshape(levels * parts * rows, width)
    odd = flags[0]
    stride = parts * rows
    for ref, scale, upward in ((far_ref, SCALE, odd), (near_ref, 1.0, 1 - odd)):
        for part in range(parts):
            for k in range(REACH):
                for f in range(fields):
                    start = (f * levels * parts + part) * rows + upward * (rows - REACH) + k
                    ref[part, k * fields + f] = flat[pl.ds(start, levels, stride=stride), :] * scale
            for k in range(FACES):
                start = part * rows + upward * (rows - FACES) + k
                ref[part, REACH * fields + k] = winds[pl.ds(start, levels, stride=stride), :] * scale


def parted(x):
    *outer, rows, lons = x.shape
    return jnp.swapaxes(x.reshape(*outer, rows, PARTS, lons // PARTS), -3, -2)


def pack(flags, state, wind):
    fields, levels, parts, rows, width = state.shape
    step = levels // CHUNKS
    sent = REACH * fields + FACES
    out = jax.ShapeDtypeStruct((parts, sent, levels, width), jnp.float32)
    out_spec = pl.BlockSpec((parts, sent, step, width), lambda i, s: (0, 0, i, 0))
    return pl.pallas_call(
        pack_kernel,
        grid_spec=pltpu.PrefetchScalarGridSpec(
            num_scalar_prefetch=1,
            grid=(CHUNKS,),
            in_specs=[
                pl.BlockSpec((fields, step, parts, rows, width), lambda i, s: (0, i, 0, 0, 0)),
                pl.BlockSpec((step, parts, rows, width), lambda i, s: (i, 0, 0, 0)),
            ],
            out_specs=[out_spec, out_spec],
        ),
        out_shape=[out, out],
        name="pack",
        compiler_params=pltpu.CompilerParams(vmem_limit_bytes=60 * MIB),
        cost_estimate=pl.CostEstimate(flops=10**6, bytes_accessed=12 * 10**6, transcendentals=0),
    )(flags, state, wind)


def limited(left, right):
    return jnp.maximum(jnp.minimum(left, right), 0.0) + jnp.minimum(jnp.maximum(left, right), 0.0)


def advance(q, c, ck, positive, first, last):
    diff = {j: q[j + 1] - q[j] for j in range(first - 2, last + 2)}
    slope = {j: limited(diff[j], diff[j - 1]) for j in range(first - 1, last + 2)}
    flux = {}
    for j in range(first, last + 2):
        flux[j] = c[j] * jnp.where(positive[j], q[j - 1], q[j]) + ck[j] * jnp.where(
            positive[j], slope[j - 1], slope[j]
        )
    return {j: q[j] - (flux[j + 1] - flux[j]) for j in range(first, last + 1)}


def gelu(v):
    inner = v * (0.7978845608028654 + (0.7978845608028654 * 0.044715) * (v * v))
    half = 0.5 * v
    return (half + half * jnp.tanh(inner)).astype(jnp.bfloat16)


def advect_rows(north, inner, state_ref, wind_ref, halo_ref, adv, offset):
    fields, chunk, parts, rows, lons = state_ref.shape
    slabs = REACH * fields
    stride = parts * rows
    flat = state_ref.reshape(fields * chunk * stride, lons)
    winds = wind_ref.reshape(chunk * stride, lons)
    first = 0 if north else rows - REACH
    last = first + REACH - 1

    @pl.loop(0, parts * chunk // 8)
    def _(n):
        part = n % parts
        t = n // parts
        here = pl.ds(pl.multiple_of(t * 8, 8), 8)
        there = pl.ds(pl.multiple_of(offset + t * 8, 8), 8)
        start = (t * 8 * parts + part) * rows
        c = {}
        for j in range(first - 2, last + 4):
            if j < 0:
                c[j] = halo_ref[part, slabs + FACES + j, here, :]
            elif j < rows:
                c[j] = winds[pl.ds(start + j, 8, stride=stride), :]
            else:
                c[j] = halo_ref[part, slabs + j - rows, here, :]
        positive = {j: v > 0.0 for j, v in c.items()}
        ck = {j: 0.5 * (jnp.abs(v) - v * v) for j, v in c.items()}
        for f in range(fields):
            q = {}
            for j in range(first - REACH, last + REACH + 1):
                if j < 0:
                    q[j] = halo_ref[part, (j + REACH) * fields + f, here, :]
                elif j < rows:
                    q[j] = flat[pl.ds(f * chunk * stride + start + j, 8, stride=stride), :]
                else:
                    q[j] = halo_ref[part, (j - rows) * fields + f, here, :]
            q = advance(q, c, ck, positive, first - 2, last + 2)
            if north:
                q[-1] = q[-1] * inner
                q[-2] = q[-2] * inner
            q = advance(q, c, ck, positive, first, last)
            for j in range(REACH):
                adv[part, j, f, there, :] = q[first + j]


def main_kernel(slow, flags, state_ref, wind_ref, halo_ref, sun_ref, bias_ref, remap_ref, w1_hbm, w2_hbm, *rest):
    if slow:
        fast_ref, out_hbm, adv, x16, w1, w2, sems, result = rest
    else:
        out_ref, unscale_ref, adv, x16, w1, w2, sems = rest
        unscale_ref[0] = 1.0 / SCALE
    step_id = pl.program_id(0)
    rows = state_ref.shape[3]
    parts, reach, fields, levels, lons = adv.shape
    chunk = state_ref.shape[1]
    load_1 = pltpu.make_async_copy(w1_hbm, w1, sems.at[0])
    load_2 = pltpu.make_async_copy(w2_hbm, w2, sems.at[1])
    odd = flags[flags.shape[0] - 2]
    north = 1 - odd if slow else odd
    inner = jnp.where(flags[flags.shape[0] - 1] > 0, 1.0, 0.0)
    offset = step_id * chunk

    @pl.when(step_id == 0)
    def _():
        load_1.start()
        load_2.start()

    @pl.when((step_id < CHUNKS) & (north == 1))
    def _():
        advect_rows(True, inner, state_ref, wind_ref, halo_ref, adv, offset)

    @pl.when((step_id < CHUNKS) & (north == 0))
    def _():
        advect_rows(False, inner, state_ref, wind_ref, halo_ref, adv, offset)

    @pl.when(step_id == CHUNKS)
    def _():
        load_1.wait()
        load_2.wait()
        base = (1 - north) * (rows - reach)
        stride = parts * rows
        if slow:
            flat_out = result.reshape(fields * levels * stride, lons)
            fast_base = north * (rows - reach)
            heated = pl.ds(0, 1)
            others = pl.ds(1, fields - 1)
            store_others = pltpu.make_async_copy(result.at[others], out_hbm.at[others], sems.at[2])
            store_heated = pltpu.make_async_copy(result.at[heated], out_hbm.at[heated], sems.at[3])

        def put(part, k, f, values):
            if slow:
                start = (f * levels * parts + part) * rows + base + k
                flat_out[pl.ds(start, levels, stride=stride), :] = values
            else:
                out_ref[part, k, f] = values

        remap = remap_ref[...]
        r_high = remap.astype(jnp.bfloat16)
        r_low = (remap - r_high.astype(jnp.float32)).astype(jnp.bfloat16)
        r_all = jnp.concatenate([r_high, r_low, r_high], axis=1)
        hidden_size = w1.shape[0]
        tile = hidden_size // TILES
        pairs = [(part, pair) for part in range(parts) for pair in range(reach // 2)]

        for f in range(fields):
            for n, (part, pair) in enumerate(pairs):
                a, b = 2 * pair, 2 * pair + 1
                x = jnp.concatenate([adv[part, a, f], adv[part, b, f]], axis=1)
                high = x.astype(jnp.bfloat16)
                low = (x - high.astype(jnp.float32)).astype(jnp.bfloat16)
                stacked = jnp.concatenate([high, high, low], axis=0)
                y = jnp.dot(r_all, stacked, preferred_element_type=jnp.float32)
                x16[n, pl.ds(f * levels, levels), :] = y.astype(jnp.bfloat16)
                for k, values in ((a, y[:, :lons]), (b, y[:, lons:])):
                    if f == 0:
                        adv[part, k, 0] = values
                    else:
                        put(part, k, f, values)
        if slow:
            for part in range(parts):
                for k in range(reach):
                    for f in range(fields):
                        start = (f * levels * parts + part) * rows + fast_base + k
                        flat_out[pl.ds(start, levels, stride=stride), :] = fast_ref[part, k, f]
            store_others.start()

        for n, (part, pair) in enumerate(pairs):
            a, b = 2 * pair, 2 * pair + 1
            lit_a = flags[parts * (base + a) + part]
            lit_b = flags[parts * (base + b) + part]

            @pl.when(lit_a + lit_b > 0)
            def _():
                inputs = x16[n]

                def layer(t):
                    z = jnp.dot(w1[pl.ds(t * tile, tile), :], inputs,
                                preferred_element_type=jnp.float32)
                    wide = bias_ref[pl.ds(t * tile, tile), :]
                    return z + jnp.concatenate([wide, wide], axis=1)

                net = jnp.zeros((levels, 2 * lons), jnp.float32)
                z = layer(0)
                for t in range(TILES):
                    later = layer(t + 1) if t < TILES - 1 else None
                    net = net + jnp.dot(w2[:, pl.ds(t * tile, tile)], gelu(z),
                                        preferred_element_type=jnp.float32)
                    z = later
                for k, lit, values in ((a, lit_a, net[:, :lons]), (b, lit_b, net[:, lons:])):
                    sun = sun_ref[part, pl.ds(base + k, 1), :]
                    weight = sun * jnp.where(lit > 0, 1.0, 0.0)
                    adv[part, k, 0] = adv[part, k, 0] + weight * values

        for part in range(parts):
            for k in range(reach):
                put(part, k, 0, adv[part, k, 0])
        if slow:
            store_heated.start()
            store_others.wait()
            store_heated.wait()


def compute(slow, flags, state, wind, halo, sunlight, bias, remap, w1, w2, fast=None):
    fields, levels, parts, rows, width = state.shape
    step = levels // CHUNKS
    last = CHUNKS - 1
    any_spec = pl.BlockSpec(memory_space=pl.ANY)
    in_specs = [
        pl.BlockSpec((fields, step, parts, rows, width), lambda i, s: (0, jnp.minimum(i, last), 0, 0, 0)),
        pl.BlockSpec((step, parts, rows, width), lambda i, s: (jnp.minimum(i, last), 0, 0, 0)),
        pl.BlockSpec((parts, halo.shape[1], step, width), lambda i, s: (0, 0, jnp.minimum(i, last), 0)),
        pl.BlockSpec(sunlight.shape, lambda i, s: (0, 0, 0)),
        pl.BlockSpec(bias.shape, lambda i, s: (0, 0)),
        pl.BlockSpec(remap.shape, lambda i, s: (0, 0)),
        any_spec,
        any_spec,
    ]
    operands = [flags, state, wind, halo, sunlight, bias, remap, w1, w2]
    kept = (parts, REACH, fields, levels, width)
    scratch = [
        pltpu.VMEM(kept, jnp.float32),
        pltpu.VMEM((parts * REACH // 2, fields * levels, 2 * width), jnp.bfloat16),
        pltpu.VMEM(w1.shape, jnp.bfloat16),
        pltpu.VMEM(w2.shape, jnp.bfloat16),
        pltpu.SemaphoreType.DMA((4,)),
    ]
    if slow:
        in_specs.append(pl.BlockSpec(kept, lambda i, s: (0, 0, 0, 0, 0)))
        operands.append(fast)
        out_spec = any_spec
        out_shape = jax.ShapeDtypeStruct(state.shape, jnp.float32)
        scratch.append(pltpu.VMEM(state.shape, jnp.float32))
    else:
        out_spec = [
            pl.BlockSpec(kept, lambda i, s: (0, 0, 0, 0, 0)),
            pl.BlockSpec(memory_space=pltpu.SMEM),
        ]
        out_shape = [
            jax.ShapeDtypeStruct(kept, jnp.float32),
            jax.ShapeDtypeStruct((1,), jnp.float32),
        ]
    return pl.pallas_call(
        functools.partial(main_kernel, slow),
        grid_spec=pltpu.PrefetchScalarGridSpec(
            num_scalar_prefetch=1,
            grid=(CHUNKS + 1,),
            in_specs=in_specs,
            out_specs=out_spec,
            scratch_shapes=scratch,
        ),
        out_shape=out_shape,
        name="slow_rows" if slow else "fast_rows",
        compiler_params=pltpu.CompilerParams(vmem_limit_bytes=56 * MIB),
        cost_estimate=pl.CostEstimate(flops=4 * 10**9, bytes_accessed=12 * 10**6, transcendentals=2 * 10**6),
    )(*operands)


def shards(state, wind, sunlight, day_list, w_first, bias, w_second, remap):
    count = lax.axis_size("lat")
    near = [(i, i ^ 1) for i in range(count) if i ^ 1 < count]
    far = [(i, i + 1) for i in range(1, count - 1, 2)]
    far = far + [(j, i) for i, j in far]
    index = lax.axis_index("lat")
    blocks = day_list.shape[1]
    block_ids = jnp.arange(blocks, dtype=jnp.int32)
    lit = jnp.any(day_list[0][None, :] == block_ids[:, None], axis=1).astype(jnp.int32)
    odd = (index % 2).astype(jnp.int32)
    inner = (index > 0).astype(jnp.int32)
    flags = jnp.concatenate([lit, odd[None], inner[None]])
    side = jnp.stack([odd, inner])
    parts_state, parts_wind = parted(state), parted(wind)
    near_sent, far_sent = pack(side, parts_state, parts_wind)
    far_halo = lax.ppermute(far_sent.astype(jnp.float16), "lat", far)
    near_halo = lax.ppermute(near_sent, "lat", near)
    w1, w2 = w_first.T, w_second.T
    wide_bias = jnp.broadcast_to(bias[:, None], (bias.shape[0], state.shape[3] // PARTS))
    shared = (parted(sunlight), wide_bias, remap, w1, w2)
    fast, unscale = compute(False, flags, parts_state, parts_wind, near_halo, *shared)
    far_halo = far_halo.astype(jnp.float32) * unscale[0]
    out = compute(True, flags, parts_state, parts_wind, far_halo, *shared, fast=fast)
    return jnp.swapaxes(out, 2, 3).reshape(state.shape)


def solution(mesh):
    placed = (
        P("member", None, "lat", None),
        P("member", "lat", None),
        P(("member", "lat"), None),
        P(("member", "lat"), None),
        P(),
        P(),
        P(),
        P(),
    )
    return jax.shard_map(
        shards,
        mesh=mesh,
        in_specs=placed,
        out_specs=P("member", None, "lat", None),
        check_vma=False,
    )
```

time: 66 us -> 74.7 us (1.13)
  waiting for transfers between devices: 0.01 us -> 9.54 us
  local copies, waits for them, and re-layouts: 12.9 us -> 4.92 us
  Pallas kernels: 39.5 us -> 45.7 us
  other arithmetic: 6.07 us -> 8.85 us
  starting transfers between devices: 6.59 us -> 4.61 us
    ppermute x2 -> x1, waiting for transfers between devices: 0.01 us -> 9.54 us  [shards(): far_halo = lax.ppermute(far_sent.astype(jnp.float16), 'lat', far)]
    unnamed x20 -> x10, local copies, waits for them, and re-layouts: 12.5 us -> 3.62 us
    pallas_call x3 -> x2, Pallas kernels: 34.3 us -> 38.3 us  [compute(): pl.pallas_call(functools.partial(main_kernel, slow), grid_spec=pltpu.Pref...]
    pallas_call x1, Pallas kernels: 5.2 us -> 7.46 us  [pack(): pl.pallas_call(pack_kernel, grid_spec=pltpu.PrefetchScalarGridSpec(num_sc...]
    ppermute x2 -> x1, starting transfers between devices: 6.51 us -> 4.49 us  [shards(): far_halo = lax.ppermute(far_sent.astype(jnp.float16), 'lat', far)]
    convert_element_type x2 -> x1, other arithmetic: 2.05 us -> 3.57 us  [shards(): far_halo = lax.ppermute(far_sent.astype(jnp.float16), 'lat', far)]
    broadcast_in_dim x1, local copies, waits for them, and re-layouts: 0.33 us -> 1.29 us  [shards(): jnp.broadcast_to(bias[:, None], (bias.shape[0], state.shape[3] // PARTS))]
    mul x2 -> x1, other arithmetic: 3.74 us -> 3.98 us  [shards(): far_halo = far_halo.astype(jnp.float32) * unscale[0]]
  transfers between devices with their start and end apart: 3 -> 2, of which waited for: 0 -> 1; matrix products, arithmetic and copies ran while one was open for 12% -> 12% of each run, Pallas kernels for 39% -> 24%
where the time goes in v1:
time: 74.7 us; the launch traced here: 73.9 us
  Pallas kernels  45.7 us (61%)
  waiting for transfers between devices  9.54 us (13%)
  other arithmetic  8.85 us (12%)
  local copies, waits for them, and re-layouts  4.92 us (7%)
  starting transfers between devices  4.61 us (6%)
    pallas_call x2, Pallas kernels, compute(): pl.pallas_call(functools.partial(main_kernel, slow), grid_spec=pltpu.Pref...  38.3 us
    ppermute x1, waiting for transfers between devices, shards(): far_halo = lax.ppermute(far_sent.astype(jnp.float16), 'lat', far)  9.54 us
    pallas_call x1, Pallas kernels, pack(): pl.pallas_call(pack_kernel, grid_spec=pltpu.PrefetchScalarGridSpec(num_sc...  7.46 us
    ppermute x1, starting transfers between devices, shards(): far_halo = lax.ppermute(far_sent.astype(jnp.float16), 'lat', far)  4.49 us
    mul x1, other arithmetic, shards(): far_halo = far_halo.astype(jnp.float32) * unscale[0]  3.98 us
    unnamed x10, local copies, waits for them, and re-layouts  3.62 us
    convert_element_type x1, other arithmetic, shards(): far_halo = lax.ppermute(far_sent.astype(jnp.float16), 'lat', far)  3.57 us
  transfers between devices with their start and end apart: 2, of which 1 were waited for; matrix products, arithmetic and copies ran while one was open for 12% of the time, Pallas kernels for 24%

profile of v1, /device:TPU:1, one launch (start us, length us, event | category | flops | bytes accessed | tf_op | source)
XLA Modules:
  0.0 73.9 jit_solution(7688898874631170425)
XLA Ops:
  0.0 0.6 pad_add_fusion.1.flags
  0.6 7.5 %pack.1 = (f32[2,23,128,128]{3,2,1,0:T(8,128)}, f32[2,23,128,128]{3,2,1,0:T(8,128)}) custom-call(s32[2]{0:T(128)} %pad_add_fusion.1.flags, f32[5,128,2,8,128]{4,3,2,1,0:T(8,128)} %bitcast.18, f32[128,2,8,128]{3,2,1,0:T(8,128)} %bitcast.23), custom_call_target="tpu_custom_call" | custom-call | flops 1000000 | bytes 12000000 | tf_op jit(solution)/shard_map/pack/pallas_call | solution.py:48
  8.0 0.0 copy-start.3
  8.0 0.0 copy-start.1
  8.0 0.0 copy-start
  8.0 0.1 collective-permute-start.1
  8.2 3.6 %convert_element_type.11 = f16[2,23,128,128]{3,2,1,0:T(8,128)(2,1)} convert(f32[2,23,128,128]{3,2,1,0:T(8,128)} %get-tuple-element.9) | non-fusion elementwise | flops 753664 | bytes 4521984 | tf_op jit(solution)/shard_map/convert_element_type | solution.py:318
  11.7 4.5 %collective-permute-start = (f16[2,23,128,128]{3,2,1,0:T(8,128)(2,1)}, f16[2,23,128,128]{3,2,1,0:T(8,128)(2,1)}, u32[]{:S(2)}, u32[]{:S(2)}) collective-permute-start(f16[2,23,128,128]{3,2,1,0:T(8,128)(2,1)} %convert_element_type.11), channel_id=1, source_target_pairs={{1,2},{3,4},{5,6},{7,8},{9,10},{11,12},{13,14},{2,1},{4,3},{6,5},{... | collective-permute-start | bytes 4521992 | tf_op jit(solution)/shard_map/ppermute | solution.py:318
  16.2 0.0 copy-done.3
  16.3 0.1 fusion
  16.4 0.0 copy-done.1
  16.4 0.0 copy-start.2
  16.4 1.0 %copy.12 = bf16[2048,128]{0,1:T(8,128)(2,1)} copy(bf16[2048,128]{1,0:T(8,128)(2,1)S(1)} %copy-done.1) | data formatting | bytes 1048576 | tf_op args[6]
  17.4 0.0 copy-done
  17.4 2.6 %copy.11 = bf16[640,2048]{0,1:T(8,128)(2,1)} copy(bf16[640,2048]{1,0:T(8,128)(2,1)S(1)} %copy-done) | data formatting | bytes 5242880 | tf_op args[4]
  20.0 0.6 pad_add_fusion.flags
  20.6 0.0 collective-permute-done.1.halo_ref
  20.6 0.0 copy-done.2
  20.6 1.3 %broadcast_in_dim.19.bias_ref = f32[2048,128]{1,0:T(8,128)} broadcast(f32[2048]{0:T(1024)S(1)} %copy-done.2), dimensions={0} | broadcast | bytes 1056768 | tf_op jit(solution)/shard_map/broadcast_in_dim | solution.py:321
  21.9 17.9 %fast_rows.1 = (f32[2,4,5,128,128]{4,3,2,1,0:T(8,128)}, f32[1]{0:T(128)}) custom-call(s32[18]{0:T(128)} %pad_add_fusion.flags, f32[5,128,2,8,128]{4,3,2,1,0:T(8,128)} %bitcast.19, f32[128,2,8,128]{3,2,1,0:T(8,128)} %bitcast.24, f32[2,23,128,128]{3,2,1,0:T(8,128)} %collective-permute-done.1.halo_ref, f32[2,8,128]{2,1,0:T(8,128)} %bitcast.28, ...), custom_call_target="tpu_custom_call" | custom-call | flops 4000000000 | bytes 12000000 | tf_op jit(solution)/shard_map/fast_rows/pallas_call | solution.py:287
  39.8 9.5 %collective-permute-done = f16[2,23,128,128]{3,2,1,0:T(8,128)(2,1)} collective-permute-done((f16[2,23,128,128]{3,2,1,0:T(8,128)(2,1)}, f16[2,23,128,128]{3,2,1,0:T(8,128)(2,1)}, u32[]{:S(2)}, u32[]{:S(2)}) %collective-permute-start) | collective-permute-done | bytes 1507360 | tf_op jit(solution)/shard_map/ppermute | solution.py:318
  49.3 4.0 %convert_multiply_fusion.halo_ref = f32[2,23,128,128]{3,2,1,0:T(8,128)} fusion(f16[2,23,128,128]{3,2,1,0:T(8,128)(2,1)} %collective-permute-done, f32[]{:T(128)} %bitcast.13), kind=kLoop, calls=%fused_computation | loop fusion | flops 1507328 | bytes 4521988 | tf_op jit(solution)/shard_map/mul | solution.py:324
  53.3 20.4 %slow_rows.1 = f32[5,128,2,8,128]{4,3,2,1,0:T(8,128)} custom-call(s32[18]{0:T(128)} %pad_add_fusion.flags, f32[5,128,2,8,128]{4,3,2,1,0:T(8,128)} %bitcast.20, f32[128,2,8,128]{3,2,1,0:T(8,128)} %bitcast.25, f32[2,23,128,128]{3,2,1,0:T(8,128)} %convert_multiply_fusion.halo_ref, f32[2,8,128]{2,1,0:T(8,128)} %bitcast.29, ...), custom_call_target="tpu_custom_call" | custom-call | flops 4000000000 | bytes 12000000 | tf_op jit(solution)/shard_map/slow_rows/pallas_call | solution.py:287
  (1 shorter events, 0.0 us)
Async XLA Ops:
  8.0 8.2 %copy-start.3 = (s32[1,16]{1,0:T(1,128)S(1)}, s32[1,16]{1,0:T(1,128)}, u32[]{:S(2)}) copy-start(s32[1,16]{1,0:T(1,128)} %param.11) | copy-start | bytes 196
  8.0 8.3 %copy-start.1 = (bf16[2048,128]{1,0:T(8,128)(2,1)S(1)}, bf16[2048,128]{1,0:T(8,128)(2,1)}, u32[]{:S(2)}) copy-start(bf16[2048,128]{1,0:T(8,128)(2,1)} %param.14) | copy-start | bytes 1572868
  8.0 9.4 %copy-start = (bf16[640,2048]{1,0:T(8,128)(2,1)S(1)}, bf16[640,2048]{1,0:T(8,128)(2,1)}, u32[]{:S(2)}) copy-start(bf16[640,2048]{1,0:T(8,128)(2,1)} %param.12) | copy-start | bytes 7864324
  8.0 12.6 %collective-permute-start.1 = (f32[2,23,128,128]{3,2,1,0:T(8,128)}, f32[2,23,128,128]{3,2,1,0:T(8,128)}, u32[]{:S(2)}, u32[]{:S(2)}) collective-permute-start(f32[2,23,128,128]{3,2,1,0:T(8,128)} %get-tuple-element.10), channel_id=1, source_target_pairs={{0,1},{1,0},{2,3},{3,2},{4,5},{5,4},{6,7},{7,6},{8,9},{9,8},{10,11... | collective-permute-start | bytes 9043976 | tf_op jit(solution)/shard_map/ppermute | solution.py:319
  11.7 37.6 %collective-permute-start = (f16[2,23,128,128]{3,2,1,0:T(8,128)(2,1)}, f16[2,23,128,128]{3,2,1,0:T(8,128)(2,1)}, u32[]{:S(2)}, u32[]{:S(2)}) collective-permute-start(f16[2,23,128,128]{3,2,1,0:T(8,128)(2,1)} %convert_element_type.11), channel_id=1, source_target_pairs={{1,2},{3,4},{5,6},{7,8},{9,10},{11,12},{13,14},{2,1},{4,3},{6,5},{... | collective-permute-start | bytes 4521992 | tf_op jit(solution)/shard_map/ppermute | solution.py:318
  16.4 4.2 %copy-start.2 = (f32[2048]{0:T(1024)S(1)}, f32[2048]{0:T(1024)}, u32[]{:S(2)}) copy-start(f32[2048]{0:T(1024)} %param.13) | copy-start | bytes 24580

commit v2 on v0

--- a/solution.py
+++ b/solution.py
@@ -85,7 +85,7 @@
         ]
         + [jax.ShapeDtypeStruct((sent, levels, width), jnp.float32)] * PARTS,
         name="pack",
-        compiler_params=pltpu.CompilerParams(vmem_limit_bytes=24 * MIB),
+        compiler_params=pltpu.CompilerParams(vmem_limit_bytes=14 * MIB),
         cost_estimate=pl.CostEstimate(flops=10**6, bytes_accessed=18 * 10**6, transcendentals=0),
     )(flags, parted(state), parted(wind))
 
@@ -333,7 +333,7 @@
         out_shape=out_shape,
         input_output_aliases=aliases,
         name="slow_rows" if slow else "fast_rows",
-        compiler_params=pltpu.CompilerParams(vmem_limit_bytes=36 * MIB),
+        compiler_params=pltpu.CompilerParams(vmem_limit_bytes=22 * MIB),
         cost_estimate=pl.CostEstimate(
             flops=2 * 10**9 * halves, bytes_accessed=6 * 10**6 * halves, transcendentals=10**6 * halves
         ),

time: 66 us -> 66.4 us (level)
  no operation moved by 1% of the time
where the time goes in v2:
time: 66.4 us; the launch traced here: 65.2 us
  Pallas kernels  39.5 us (59%)
  local copies, waits for them, and re-layouts  12.9 us (19%)
  starting transfers between devices  6.59 us (10%)
  other arithmetic  6.07 us (9%)
    pallas_call x3, Pallas kernels, compute(): pl.pallas_call(functools.partial(main_kernel, slow, part, rows), grid_spe...  34.3 us
    unnamed x20, local copies, waits for them, and re-layouts  12.5 us
    ppermute x2, starting transfers between devices, shards(): lax.ppermute(sent.astype(jnp.float16), 'lat', far)  6.51 us
    pallas_call x1, Pallas kernels, pack(): pl.pallas_call(pack_kernel, grid_spec=pltpu.PrefetchScalarGridSpec(num_sc...  5.2 us
    mul x2, other arithmetic, shards(): halo = far_halos[part].astype(jnp.float32) * unscale[0]  3.74 us
    convert_element_type x2, other arithmetic, shards(): sent.astype(jnp.float16)  2.05 us
  transfers between devices with their start and end apart: 3, of which 0 were waited for; matrix products, arithmetic and copies ran while one was open for 12% of the time, Pallas kernels for 39%

profile of v2, /device:TPU:1, one launch (start us, length us, event | category | flops | bytes accessed | tf_op | source)
XLA Modules:
  0.0 65.2 jit_solution(11306731095414152518)
XLA Ops:
  0.0 0.1 pad_add_fusion.1.flags
  0.1 0.0 copy-start.2
  0.1 2.5 %copy-done.2 = f32[5,128,8,256]{3,2,1,0:T(8,128)S(1)} copy-done((f32[5,128,8,256]{3,2,1,0:T(8,128)S(1)}, f32[5,128,8,256]{3,2,1,0:T(8,128)}, u32[]{:S(2)}) %copy-start.2) | copy-done | bytes 5242904
  2.6 0.0 copy-start.3
  2.6 1.2 %copy-done.3 = f32[128,8,256]{2,1,0:T(8,128)S(1)} copy-done((f32[128,8,256]{2,1,0:T(8,128)S(1)}, f32[128,8,256]{2,1,0:T(8,128)}, u32[]{:S(2)}) %copy-start.3) | copy-done | bytes 1048600
  3.8 5.2 %pack.1 = (f32[2,48,128,128]{3,2,1,0:T(8,128)S(1)}, f32[2,23,128,128]{3,2,1,0:T(8,128)}, f32[23,128,128]{2,1,0:T(8,128)S(1)}, f32[23,128,128]{2,1,0:T(8,128)S(1)}) custom-call(s32[2]{0:T(128)S(1)} %pad_add_fusion.1.flags, f32[5,128,2,8,128]{4,3,2,1,0:T(8,128)S(1)} %bitcast.15, f32[128,2,8,128]{3,2,1,0:T(8,128)S(1)} %bitcast.19), custom_call_target="tpu_custom_call" | custom-call | flops 1000000 | bytes 18000000 | tf_op jit(solution)/shard_map/pack/pallas_call | solution.py:67
  9.0 0.0 copy-start
  9.0 2.7 %copy-done = f32[2,48,128,128]{3,2,1,0:T(8,128)} copy-done((f32[2,48,128,128]{3,2,1,0:T(8,128)}, f32[2,48,128,128]{3,2,1,0:T(8,128)S(1)}, u32[]{:S(2)}) %copy-start) | copy-done | bytes 6291480
  11.6 0.1 collective-permute-start.1
  11.7 1.0 %convert_element_type.19 = f16[23,128,128]{2,1,0:T(8,128)(2,1)} convert(f32[23,128,128]{2,1,0:T(8,128)S(1)} %get-tuple-element.16) | non-fusion elementwise | flops 376832 | bytes 2260992 | tf_op jit(solution)/shard_map/convert_element_type | solution.py:357
  12.8 0.0 copy-start.8
  12.8 0.0 copy-start.6
  12.8 4.6 %collective-permute-start.2 = (f16[23,128,128]{2,1,0:T(8,128)(2,1)}, f16[23,128,128]{2,1,0:T(8,128)(2,1)}, u32[]{:S(2)}, u32[]{:S(2)}) collective-permute-start(f16[23,128,128]{2,1,0:T(8,128)(2,1)} %convert_element_type.19), channel_id=1, source_target_pairs={{1,2},{3,4},{5,6},{7,8},{9,10},{11,12},{13,14},{2,1},{4,3},{6,5},{... | collective-permute-start | bytes 2261000 | tf_op jit(solution)/shard_map/ppermute | solution.py:357
  17.4 1.0 %convert_element_type.17 = f16[23,128,128]{2,1,0:T(8,128)(2,1)} convert(f32[23,128,128]{2,1,0:T(8,128)S(1)} %get-tuple-element.12) | non-fusion elementwise | flops 376832 | bytes 2260992 | tf_op jit(solution)/shard_map/convert_element_type | solution.py:357
  18.4 1.9 %collective-permute-start = (f16[23,128,128]{2,1,0:T(8,128)(2,1)}, f16[23,128,128]{2,1,0:T(8,128)(2,1)}, u32[]{:S(2)}, u32[]{:S(2)}) collective-permute-start(f16[23,128,128]{2,1,0:T(8,128)(2,1)} %convert_element_type.17), channel_id=1, source_target_pairs={{1,2},{3,4},{5,6},{7,8},{9,10},{11,12},{13,14},{2,1},{4,3},{6,5},{... | collective-permute-start | bytes 2261000 | tf_op jit(solution)/shard_map/ppermute | solution.py:357
  20.3 0.0 copy-done.8
  20.3 0.1 fusion
  20.4 0.0 copy-done.6
  20.4 0.2 copy.13
  20.7 0.0 copy-start.7
  20.7 0.0 copy-start.4
  20.7 0.0 copy-start.5
  20.7 3.2 %copy.12 = bf16[640,2048]{0,1:T(8,128)(2,1)S(1)} copy(bf16[640,2048]{1,0:T(8,128)(2,1)} %param.12) | data formatting | bytes 5242880 | tf_op args[4]
  23.9 0.1 pad_add_fusion.flags
  24.0 0.0 collective-permute-done.1.halo_ref
  24.0 0.0 copy-done.7
  24.0 0.3 broadcast_in_dim.19.bias_ref
  24.3 0.0 copy-done.4
  24.3 0.0 copy-done.5
  24.3 0.0 copy-start.1
  24.3 2.8 %copy-done.1 = f32[2,48,128,128]{3,2,1,0:T(8,128)S(1)} copy-done((f32[2,48,128,128]{3,2,1,0:T(8,128)S(1)}, f32[2,48,128,128]{3,2,1,0:T(8,128)}, u32[]{:S(2)}) %copy-start.1) | copy-done | bytes 6291480
  27.1 16.6 %fast_rows.1 = (f32[2,4,5,128,128]{4,3,2,1,0:T(8,128)S(1)}, f32[1]{0:T(128)}) custom-call(s32[18]{0:T(128)S(1)} %pad_add_fusion.flags, f32[2,48,128,128]{3,2,1,0:T(8,128)S(1)} %copy-done.1, f32[2,23,128,128]{3,2,1,0:T(8,128)} %collective-permute-done.1.halo_ref, f32[8,256]{1,0:T(8,128)S(1)} %copy-done.5, f32[2048,128]{1,0:T(8,128)S(1)} %broadcast_in_dim.19.bias_ref, ...), custom_call_target="tpu_custom_call" | custom-call | flops 4000000000 | bytes 12000000 | tf_op jit(solution)/shard_map/fast_rows/pallas_call | solution.py:324
  43.8 0.0 collective-permute-done.2
  43.8 1.9 %convert_multiply_fusion.halo_ref = f32[23,128,128]{2,1,0:T(8,128)S(1)} fusion(f16[23,128,128]{2,1,0:T(8,128)(2,1)} %collective-permute-done.2, f32[]{:T(128)} %bitcast.9), kind=kLoop, calls=%fused_computation | loop fusion | flops 753664 | bytes 2260996 | tf_op jit(solution)/shard_map/mul | solution.py:365
  45.6 8.8 %slow_rows.2.rest_1_ = f32[5,128,8,256]{3,2,1,0:T(8,128)} custom-call(s32[18]{0:T(128)S(1)} %pad_add_fusion.flags, f32[2,48,128,128]{3,2,1,0:T(8,128)S(1)} %copy-done.1, f32[23,128,128]{2,1,0:T(8,128)S(1)} %convert_multiply_fusion.halo_ref, f32[8,256]{1,0:T(8,128)S(1)} %copy-done.5, f32[2048,128]{1,0:T(8,128)S(1)} %broadcast_in_dim.19.bias_ref, ...), custom_call_target="tpu_custom_call" | custom-call | flops 2000000000 | bytes 6000000 | tf_op jit(solution)/shard_map/slow_rows/pallas_call | solution.py:324
  54.5 0.0 collective-permute-done
  54.5 1.9 %convert_multiply_fusion.1.halo_ref = f32[23,128,128]{2,1,0:T(8,128)S(1)} fusion(f16[23,128,128]{2,1,0:T(8,128)(2,1)} %collective-permute-done, f32[]{:T(128)} %bitcast.9), kind=kLoop, calls=%fused_computation.1 | loop fusion | flops 753664 | bytes 2260996 | tf_op jit(solution)/shard_map/mul | solution.py:365
  56.4 8.8 %slow_rows.3 = f32[5,128,8,256]{3,2,1,0:T(8,128)} custom-call(s32[18]{0:T(128)S(1)} %pad_add_fusion.flags, f32[2,48,128,128]{3,2,1,0:T(8,128)S(1)} %copy-done.1, f32[23,128,128]{2,1,0:T(8,128)S(1)} %convert_multiply_fusion.1.halo_ref, f32[8,256]{1,0:T(8,128)S(1)} %copy-done.5, ...), custom_call_target="tpu_custom_call", output_to_operand_aliasing={{}: (9, {})} | custom-call | flops 2000000000 | bytes 6000000 | tf_op jit(solution)/shard_map/slow_rows/pallas_call | solution.py:324
  (1 shorter events, 0.0 us)
Async XLA Ops:
  0.1 2.5 %copy-start.2 = (f32[5,128,8,256]{3,2,1,0:T(8,128)S(1)}, f32[5,128,8,256]{3,2,1,0:T(8,128)}, u32[]{:S(2)}) copy-start(f32[5,128,8,256]{3,2,1,0:T(8,128)} %param.8) | copy-start | bytes 15728644
  2.6 1.2 %copy-start.3 = (f32[128,8,256]{2,1,0:T(8,128)S(1)}, f32[128,8,256]{2,1,0:T(8,128)}, u32[]{:S(2)}) copy-start(f32[128,8,256]{2,1,0:T(8,128)} %param.9) | copy-start | bytes 3145732
  9.0 2.7 %copy-start = (f32[2,48,128,128]{3,2,1,0:T(8,128)}, f32[2,48,128,128]{3,2,1,0:T(8,128)S(1)}, u32[]{:S(2)}) copy-start(f32[2,48,128,128]{3,2,1,0:T(8,128)S(1)} %get-tuple-element.11.own_ref) | copy-start | bytes 18874372
  11.6 12.3 %collective-permute-start.1 = (f32[2,23,128,128]{3,2,1,0:T(8,128)}, f32[2,23,128,128]{3,2,1,0:T(8,128)}, u32[]{:S(2)}, u32[]{:S(2)}) collective-permute-start(f32[2,23,128,128]{3,2,1,0:T(8,128)} %get-tuple-element.13), channel_id=1, source_target_pairs={{0,1},{1,0},{2,3},{3,2},{4,5},{5,4},{6,7},{7,6},{8,9},{9,8},{10,11... | collective-permute-start | bytes 9043976 | tf_op jit(solution)/shard_map/ppermute | solution.py:358
  12.8 7.6 %copy-start.8 = (s32[1,16]{1,0:T(1,128)S(1)}, s32[1,16]{1,0:T(1,128)}, u32[]{:S(2)}) copy-start(s32[1,16]{1,0:T(1,128)} %param.11) | copy-start | bytes 196
  12.8 7.7 %copy-start.6 = (bf16[2048,128]{1,0:T(8,128)(2,1)S(1)}, bf16[2048,128]{1,0:T(8,128)(2,1)}, u32[]{:S(2)}) copy-start(bf16[2048,128]{1,0:T(8,128)(2,1)} %param.14) | copy-start | bytes 1572868
  12.8 31.0 %collective-permute-start.2 = (f16[23,128,128]{2,1,0:T(8,128)(2,1)}, f16[23,128,128]{2,1,0:T(8,128)(2,1)}, u32[]{:S(2)}, u32[]{:S(2)}) collective-permute-start(f16[23,128,128]{2,1,0:T(8,128)(2,1)} %convert_element_type.19), channel_id=1, source_target_pairs={{1,2},{3,4},{5,6},{7,8},{9,10},{11,12},{13,14},{2,1},{4,3},{6,5},{... | collective-permute-start | bytes 2261000 | tf_op jit(solution)/shard_map/ppermute | solution.py:357
  18.4 36.1 %collective-permute-start = (f16[23,128,128]{2,1,0:T(8,128)(2,1)}, f16[23,128,128]{2,1,0:T(8,128)(2,1)}, u32[]{:S(2)}, u32[]{:S(2)}) collective-permute-start(f16[23,128,128]{2,1,0:T(8,128)(2,1)} %convert_element_type.17), channel_id=1, source_target_pairs={{1,2},{3,4},{5,6},{7,8},{9,10},{11,12},{13,14},{2,1},{4,3},{6,5},{... | collective-permute-start | bytes 2261000 | tf_op jit(solution)/shard_map/ppermute | solution.py:357
  20.7 3.3 %copy-start.7 = (f32[2048]{0:T(1024)S(1)}, f32[2048]{0:T(1024)}, u32[]{:S(2)}) copy-start(f32[2048]{0:T(1024)} %param.13) | copy-start | bytes 24580
  20.7 3.6 %copy-start.4 = (f32[128,128]{1,0:T(8,128)S(1)}, f32[128,128]{1,0:T(8,128)}, u32[]{:S(2)}) copy-start(f32[128,128]{1,0:T(8,128)} %remap_ref.5) | copy-start | bytes 196612
  20.7 3.6 %copy-start.5 = (f32[8,256]{1,0:T(8,128)S(1)}, f32[8,256]{1,0:T(8,128)}, u32[]{:S(2)}) copy-start(f32[8,256]{1,0:T(8,128)} %sun_ref.5) | copy-start | bytes 24580
  24.3 2.8 %copy-start.1 = (f32[2,48,128,128]{3,2,1,0:T(8,128)S(1)}, f32[2,48,128,128]{3,2,1,0:T(8,128)}, u32[]{:S(2)}) copy-start(f32[2,48,128,128]{3,2,1,0:T(8,128)} %copy-done) | copy-start | bytes 18874372
